TPU v7x, 256 devices: a whole 4x4x8 slice. The times are simulated.
256 devices in a mesh: dp: 4 (over y), expert: 64 (over x, z, core).
Axes of the slice: x: 4, y: 4, z: 8, core: 2. Of those that a mesh axis runs over, the one named last changes fastest.
Arguments:
- tokens: bfloat16 [6144, 4096], P(('dp', 'expert')), may hold values from -6 to 6
- route_ids: int32 [6144, 8], P(('dp', 'expert')), may hold values from 0 to 127, as said below
- route_weights: float32 [6144, 8], P(('dp', 'expert')), may hold values from 0.05 to 1
- placement: int32 [128], replicated, may hold values from 0 to 127, each once
- gate_up: bfloat16 [128, 4096, 1536], P('expert', None, 'dp'), may hold values from -0.09375 to 0.09375
- down: bfloat16 [128, 768, 4096], P('expert', None, 'dp'), may hold values from -0.21875 to 0.21875
- queries: bfloat16 [1024, 4, 8192], P(('dp', 'expert')), may hold values from -12 to 12
- draft_keys: bfloat16 [1024, 4, 512], P(('dp', 'expert')), may hold values from -4 to 4
- draft_values: bfloat16 [1024, 4, 512], P(('dp', 'expert')), may hold values from -6 to 6
- cache_keys: bfloat16 [1024, 256, 512], P(('dp', 'expert')), may hold values from -4 to 4
- cache_values: bfloat16 [1024, 256, 512], P(('dp', 'expert')), may hold values from -6 to 6
- cache_lengths: int32 [1024], P(('dp', 'expert')), may hold values from 1 to 256, 131072 in all
Outputs:
- mixed: bfloat16 [6144, 4096], P(('dp', 'expert'))
- context: bfloat16 [1024, 4, 8192], P(('dp', 'expert'))
Inputs may be any that keep to these rules, and one draw needn't show every extreme that they name: `route_ids`: each row names 8 different experts. 2 experts, the same for the whole step, are each named by exactly 4 of the rows of every device; every other expert by 1 or 2 rows of each device, and one of them by 2 rows of every device. `placement`: each slot holds one expert; slot s lies on index s // 2 of expert. `cache_lengths`: the lengths of all requests sum to 131072.
All inputs are finite; a program needn't handle non-finite values. No bound on the sum of `cache_lengths` on one device may be relied on, other than what follows from the above.
Results may differ from a plain program's by a relative error of at most 0.0057.
Values may be sent and summed in bfloat16 or wider, within the bound.
No kernel may reach another device: no remote copies, remote signals or barrier semaphores. Data moves between devices by JAX's collectives and lax.ppermute only.
A program may use at most 128 MiB of HBM per device.

v0:
```python
import math

import jax
import jax.numpy as jnp
from jax import lax
from jax.sharding import PartitionSpec as P

HEAD_DIM = 128
HOT = 2


def from_root(block, axis, owner):
    block = jnp.where(lax.axis_index(axis) == owner, block, jnp.zeros_like(block))
    return lax.psum(block, axis)


def attend_block(queries, draft_keys, draft_values, cache_keys, cache_values, cache_lengths):
    req_here, drafts, query_width = queries.shape
    context_len = cache_keys.shape[1]
    groups = draft_keys.shape[2] // HEAD_DIM
    per_group = query_width // (groups * HEAD_DIM)
    scaling = 1.0 / math.sqrt(HEAD_DIM)
    query_heads = queries.reshape(req_here, drafts, groups, per_group, HEAD_DIM)
    cache_k = cache_keys.reshape(req_here, context_len, groups, HEAD_DIM)
    cache_v = cache_values.reshape(req_here, context_len, groups, HEAD_DIM)
    draft_k = draft_keys.reshape(req_here, drafts, groups, HEAD_DIM)
    draft_v = draft_values.reshape(req_here, drafts, groups, HEAD_DIM)
    score_cache = (
        jnp.einsum("rigpe,rcge->rgpic", query_heads, cache_k, preferred_element_type=jnp.float32)
        * scaling
    )
    score_draft = (
        jnp.einsum("rigpe,rjge->rgpij", query_heads, draft_k, preferred_element_type=jnp.float32)
        * scaling
    )
    live_cache = jnp.arange(context_len, dtype=jnp.int32)[None, :] < cache_lengths[:, None]
    live_draft = (
        jnp.arange(drafts, dtype=jnp.int32)[None, :] <= jnp.arange(drafts, dtype=jnp.int32)[:, None]
    )
    score_cache = jnp.where(live_cache[:, None, None, None, :], score_cache, -1e30)
    score_draft = jnp.where(live_draft[None, None, None, :, :], score_draft, -1e30)
    highest = jnp.maximum(jnp.max(score_cache, axis=-1), jnp.max(score_draft, axis=-1))
    expo_cache = jnp.exp(score_cache - highest[..., None])
    expo_draft = jnp.exp(score_draft - highest[..., None])
    totals = jnp.sum(expo_cache, axis=-1) + jnp.sum(expo_draft, axis=-1)
    prob_cache = (expo_cache / totals[..., None]).astype(jnp.bfloat16)
    prob_draft = (expo_draft / totals[..., None]).astype(jnp.bfloat16)
    result = jnp.einsum(
        "rgpic,rcge->rigpe", prob_cache, cache_v, preferred_element_type=jnp.float32
    )
    result = result + jnp.einsum(
        "rgpij,rjge->rigpe", prob_draft, draft_v, preferred_element_type=jnp.float32
    )
    return result.astype(jnp.bfloat16).reshape(req_here, drafts, query_width)


def hidden_part(rows, gate_up):
    split_pair = gate_up.reshape(gate_up.shape[0], gate_up.shape[1], 2, gate_up.shape[2] // 2)
    projected = jnp.einsum(
        "qslcd,ldgf->qslcgf", rows, split_pair, preferred_element_type=jnp.float32
    )
    return (jax.nn.silu(projected[..., 0, :]) * projected[..., 1, :]).astype(jnp.bfloat16)


def down_part(hidden, down):
    return jnp.einsum("qslcf,lfd->qslcd", hidden, down, preferred_element_type=jnp.float32).astype(
        jnp.bfloat16
    )


def shadow_copy(gate_up, down, slot_here):
    local_slot = slot_here % gate_up.shape[0]
    owner = slot_here // gate_up.shape[0]
    gate_one = lax.dynamic_index_in_dim(gate_up, local_slot, 0, keepdims=False)
    down_one = lax.dynamic_index_in_dim(down, local_slot, 0, keepdims=False)
    return (from_root(gate_one, "expert", owner), from_root(down_one, "expert", owner))


def per_device(
    tokens,
    route_ids,
    route_weights,
    placement,
    gate_up,
    down,
    queries,
    draft_keys,
    draft_values,
    cache_keys,
    cache_values,
    cache_lengths,
):
    experts_per = gate_up.shape[0]
    n_expert = lax.axis_size("expert")
    row_count, pick_width = route_ids.shape
    experts = placement.shape[0]
    model_width = tokens.shape[1]
    hot_rows = min(row_count, 3 * row_count * pick_width // experts)
    cap_rows = (row_count * pick_width - HOT * hot_rows + experts - HOT - 1) // (experts - HOT)
    flat_ids = route_ids.reshape(-1)
    expert_range = jnp.arange(experts, dtype=jnp.int32)
    onehot = (flat_ids[:, None] == expert_range[None, :]).astype(jnp.int32)
    counts = jnp.sum(onehot, axis=0)
    slot_rank = jnp.sum((jnp.cumsum(onehot, axis=0) - onehot) * onehot, axis=1)
    slot_of = jnp.sum(onehot * placement[None, :], axis=1)
    source_rows = tokens[jnp.arange(flat_ids.shape[0], dtype=jnp.int32) // pick_width]
    ranking = counts * experts + (experts - 1 - expert_range)
    hot_ids = lax.top_k(ranking, HOT)[1]
    hot_match = (flat_ids[:, None] == hot_ids[None, :]).astype(jnp.int32)
    is_hot = jnp.sum(hot_match, axis=1) > 0
    hot_pos = jnp.where(
        is_hot,
        jnp.sum(hot_match * jnp.arange(HOT, dtype=jnp.int32)[None, :], axis=1) * hot_rows
        + slot_rank,
        HOT * hot_rows,
    )
    send_pos = jnp.where(is_hot, experts * cap_rows, slot_of * cap_rows + slot_rank)
    outgoing = (
        jnp.zeros((experts * cap_rows, model_width), jnp.bfloat16)
        .at[send_pos]
        .set(source_rows, mode="drop")
    )
    arrived = lax.all_to_all(
        outgoing.reshape(n_expert, experts_per * cap_rows, model_width),
        "expert",
        split_axis=0,
        concat_axis=0,
        tiled=True,
    )
    arrived = arrived.reshape(1, n_expert, experts_per, cap_rows, model_width)
    hot_slots = jnp.sum(
        (hot_ids[:, None] == expert_range[None, :]).astype(jnp.int32) * placement[None, :], axis=1
    )
    gate_copies = []
    down_copies = []
    for hot_index in range(HOT):
        gate_one, down_one = shadow_copy(gate_up, down, hot_slots[hot_index])
        gate_copies.append(gate_one)
        down_copies.append(down_one)
    hot_gate = jnp.stack(gate_copies)
    hot_down = jnp.stack(down_copies)
    hot_buffer = (
        jnp.zeros((HOT * hot_rows, model_width), jnp.bfloat16)
        .at[hot_pos]
        .set(source_rows, mode="drop")
    )
    gathered, gathered_hot = (
        lax.all_gather(arrived, "dp", axis=0, tiled=True),
        lax.all_gather(hot_buffer.reshape(1, HOT, hot_rows, model_width), "dp", axis=0, tiled=True),
    )
    hidden_local = hidden_part(gathered, gate_up)
    hidden_hot = hidden_part(gathered_hot[:, None], hot_gate)
    hidden_full, hidden_hot_full = (
        lax.all_gather(hidden_local, "dp", axis=4, tiled=True),
        lax.all_gather(hidden_hot, "dp", axis=4, tiled=True),
    )
    column_out = down_part(hidden_full, down)
    column_hot = down_part(hidden_hot_full, hot_down)
    back, back_hot = (
        lax.all_to_all(column_out, "dp", split_axis=0, concat_axis=4, tiled=True),
        lax.all_to_all(column_hot, "dp", split_axis=0, concat_axis=4, tiled=True),
    )
    hot_out = back_hot.reshape(HOT * hot_rows, model_width)
    expert_out = back.reshape(n_expert, experts_per * cap_rows, model_width)
    returned = lax.all_to_all(
        expert_out, "expert", split_axis=0, concat_axis=0, tiled=True
    ).reshape(experts * cap_rows, model_width)
    picked = returned[jnp.minimum(send_pos, experts * cap_rows - 1)]
    picked = jnp.where(is_hot[:, None], hot_out[jnp.minimum(hot_pos, HOT * hot_rows - 1)], picked)
    weighted = route_weights.reshape(-1)[:, None] * picked.astype(jnp.float32)
    mixed = jnp.sum(weighted.reshape(row_count, pick_width, model_width), axis=1).astype(
        jnp.bfloat16
    )
    context = attend_block(
        queries, draft_keys, draft_values, cache_keys, cache_values, cache_lengths
    )
    return (mixed, context)


def solution(mesh):
    in_specs = (
        P(("dp", "expert"), None),
        P(("dp", "expert"), None),
        P(("dp", "expert"), None),
        P(),
        P("expert", None, "dp"),
        P("expert", None, "dp"),
        P(("dp", "expert"), None, None),
        P(("dp", "expert"), None, None),
        P(("dp", "expert"), None, None),
        P(("dp", "expert"), None, None),
        P(("dp", "expert"), None, None),
        P(("dp", "expert")),
    )
    out_specs = (P(("dp", "expert"), None), P(("dp", "expert"), None, None))
    return jax.shard_map(
        per_device, mesh=mesh, in_specs=in_specs, out_specs=out_specs, check_vma=False
    )
```

profile of v0, /device:TPU:2, one launch (start us, length us, event | category | flops | bytes accessed | tf_op | source)
XLA Modules:
  0.0 524.6 jit_solution(17650561915618198852)
XLA Ops:
  8.0 0.0 all-gather.3.cloned.1.call-start
  8.1 0.8 copy.73
  8.9 0.1 eq.59
  9.0 0.1 iota_compare_fusion
  9.1 0.1 fusion.35
  9.3 0.9 select_reduce_fusion
  10.2 2.5 top_k.11
  12.7 0.1 fusion.51
  12.9 2.7 gather_fusion
  15.6 4.2 scatter_custom_fusion.1
  19.8 2.2 reshape.366
  22.0 61.6 %all_to_all.40 = bf16[64,4,4096]{2,1,0:T(4,128)(2,1)S(1)} all-to-all(bf16[64,4,4096]{2,1,0:T(4,128)(2,1)} %reshape.366), channel_id=1, replica_groups=mesh['dp'=4,'expert'=64] {'expert'}, dimensions={0} | all-to-all | bytes 4194304 | tf_op jit(solution)/shard_map/all_to_all | solution.py:123
  83.6 2.5 copy.83
  86.1 0.0 all-gather.5.cloned.1.call-start
  86.1 8.5 %copy.84 = bf16[2,4096,384]{1,2,0:T(8,128)(2,1)} copy(bf16[2,4096,384]{2,1,0:T(8,128)(2,1)} %param.16) | data formatting | bytes 12582912 | tf_op args[4]
  94.7 75.7 %all-gather.3.cloned.1.call-done = bf16[4,64,2,2,4096]{4,1,3,0,2:T(8,128)(2,1)} async-done(((bf16[1,64,2,2,4096]{4,1,3,0,2:T(8,128)(2,1)}), bf16[4,64,2,2,4096]{4,1,3,0,2:T(8,128)(2,1)}) %all-gather.3.cloned.1.call-update) | async-done | bytes 8388624 | tf_op jit(solution)/shard_map/all_gather | solution.py:148
  170.4 8.8 %fusion.11 = f32[4,64,2,2,2,192]{5,1,4,3,0,2:T(8,128)S(1)} fusion(bf16[2,4096,2,192,1,1]{1,3,2,5,4,0:T(8,128)(2,1)} %bitcast.152, bf16[4,64,2,2,4096]{4,1,3,0,2:T(8,128)(2,1)} %all-gather.3.cloned.1.call-done), kind=kOutput, calls=%fused_computation.18 | convolution fusion | flops 3221225472 | bytes 16252928 | tf_op jit(solution)/shard_map/qslcd,ldgf->qslcgf/dot_general | solution.py:59
  179.2 0.3 fusion.24
  179.5 1.3 copy.86
  180.8 0.2 all-reduce.4.cloned.1.call-start
  181.1 0.2 fusion.52
  181.3 0.6 fusion.55
  187.1 5.0 dynamic-slice_select_fusion.1
  192.1 3.0 copy.74
  195.1 5.0 copy.75
  200.1 1.9 dynamic-slice_select_fusion.3
  202.0 0.0 all-reduce.4.cloned.1.call-update
  202.0 22.1 %all-gather.5.cloned.1.call-done = bf16[4,64,2,2,768]{1,0,3,2,4:T(4,128)(2,1)} async-done(((bf16[4,64,2,2,192]{1,0,3,2,4:T(4,128)(2,1)}), bf16[4,64,2,2,768]{1,0,3,2,4:T(4,128)(2,1)}) %all-gather.5.cloned.1.call-update) | async-done | bytes 1572880 | tf_op jit(solution)/shard_map/all_gather | solution.py:154
  224.1 4.0 convert_bitcast_fusion
  228.1 1.5 copy.88
  229.6 3.6 all-to-all-start.2
  233.2 3.5 scatter_custom_fusion
  236.8 29.3 %all_gather.12 = bf16[4,2,4,4096]{3,2,0,1:T(4,128)(2,1)S(1)} all-gather(bf16[1,2,4,4096]{3,2,0,1:T(4,128)(2,1)S(1)} %reshape.363), channel_id=1, replica_groups=mesh['dp'=4,'expert'=64] {'dp'}, dimensions={0}, use_global_device_ids=true | all-gather | bytes 327680 | tf_op jit(solution)/shard_map/all_gather | solution.py:149
  266.0 144.6 %all-reduce.4.cloned.1.call-done = (bf16[1,768,1024]{2,1,0:T(8,128)(2,1)}, bf16[1,768,1024]{2,1,0:T(8,128)(2,1)}, bf16[1,4096,2,192]{1,3,2,0:T(8,128)(2,1)}, bf16[1,4096,2,192]{1,3,2,0:T(8,128)(2,1)}) async-done(((bf16[1,768,1024]{2,1,0:T(8,128)(2,1)}, bf16[1,768,1024]{2,1,0:T(8,128)(2,1)}, bf16[1,4096,2,192]{1,3,2,0:T(8,128)(2,1)}, bf16[1,4096,2,192]{1,3,2,0:T(8,128)(2,1)}), ...) | async-done | bytes 9437200 | tf_op jit(solution)/shard_map/psum | solution.py:14
  410.6 4.0 fusion.22
  414.7 0.3 copy.79
  415.0 17.8 %all_gather.13 = bf16[4,1,2,4,768]{3,0,2,1,4:T(4,128)(2,1)} all-gather(bf16[4,1,2,4,192]{3,0,2,1,4:T(4,128)(2,1)S(1)} %copy.79), channel_id=1, replica_groups=mesh['dp'=4,'expert'=64] {'dp'}, dimensions={4}, use_global_device_ids=true | all-gather | bytes 61440 | tf_op jit(solution)/shard_map/all_gather | solution.py:155
  432.8 2.9 copy.80
  435.7 2.5 fusion.21
  438.2 0.7 copy.81
  438.9 3.4 all-to-all-start
  442.3 2.9 copy.108
  445.2 4.5 reshape.432
  449.7 8.5 %all-to-all-start.3 = ((bf16[64,4,4096]{2,1,0:T(4,128)(2,1)}), bf16[64,4,4096]{2,1,0:T(4,128)(2,1)}, u32[]{:S(2)}, u32[]{:S(2)}) async-start(bf16[64,4,4096]{2,1,0:T(4,128)(2,1)} %reshape.432), calls=%async_computation.3 | async-start | bytes 4194304 | tf_op jit(solution)/shard_map/all_to_all | solution.py:165
  458.3 0.1 gt.30
  458.4 0.1 copy.72
  458.5 1.0 reshape.372
  459.5 0.3 reshape.371
  459.7 0.3 reshape.374
  460.1 0.1 copy-done.10
  460.1 0.1 iota_compare_fusion.2
  460.2 1.7 fusion.57
  461.9 1.5 fusion.56
  463.5 0.1 fusion.38
  463.6 0.4 fusion.29
  464.1 0.3 fusion.40
  464.4 0.5 fusion.17
  464.9 0.8 reshape.376
  465.7 0.1 copy.82
  465.8 2.7 gather_fusion.1
  468.4 39.3 %all-to-all-done.3 = bf16[64,4,4096]{2,1,0:T(4,128)(2,1)} async-done(((bf16[64,4,4096]{2,1,0:T(4,128)(2,1)}), bf16[64,4,4096]{2,1,0:T(4,128)(2,1)}, u32[]{:S(2)}, u32[]{:S(2)}) %all-to-all-start.3) | async-done | bytes 2097184 | tf_op jit(solution)/shard_map/all_to_all | solution.py:165
  507.7 2.5 reshape.370
  510.3 2.7 gather_fusion.2
  512.9 4.2 multiply_reduce_fusion
  (48 shorter events, 0.4 us)
Async XLA Ops:
  8.0 4.9 copy-start
  8.0 162.4 %all-gather.3.cloned.1.call-start = ((), (), s32[]{:S(2)}) async-start(), calls=%async_computation.4 | async-start | bytes 10485760 | tf_op jit(solution)/shard_map/all_gather | solution.py:148
  86.1 138.0 %all-gather.5.cloned.1.call-start = ((), (), s32[]{:S(2)}) async-start(), calls=%async_computation.5 | async-start | bytes 3932160 | tf_op jit(solution)/shard_map/all_gather | solution.py:154
  179.2 1.9 copy-start.7
  180.8 229.8 %all-reduce.4.cloned.1.call-start = ((), (), s32[]{:S(2)}) async-start(), calls=%async_computation.6 | async-start | bytes 18874368 | tf_op jit(solution)/shard_map/psum | solution.py:14
  195.1 5.0 copy-start.2
  229.6 209.3 %all-to-all-start.2 = ((bf16[4,64,2,2,1024]{4,1,3,2,0:T(8,128)(2,1)}), bf16[4,64,2,2,1024]{4,1,3,2,0:T(8,128)(2,1)S(1)}, u32[]{:S(2)}, u32[]{:S(2)}) async-start(bf16[4,64,2,2,1024]{4,1,3,2,0:T(8,128)(2,1)} %copy.88), calls=%async_computation.2 | async-start | bytes 4194304 | tf_op jit(solution)/shard_map/all_to_all | solution.py:160
  438.9 10.8 %all-to-all-start = ((bf16[4,1,2,4,1024]{4,3,2,1,0:T(4,128)(2,1)}), bf16[4,1,2,4,1024]{4,3,2,1,0:T(4,128)(2,1)S(1)}, u32[]{:S(2)}, u32[]{:S(2)}) async-start(bf16[4,1,2,4,1024]{4,3,2,1,0:T(4,128)(2,1)} %copy.81), calls=%async_computation | async-start | bytes 131072 | tf_op jit(solution)/shard_map/all_to_all | solution.py:161
  449.7 8.7 %copy-start.6 = (f32[24,8]{0,1:T(8,128)S(1)}, f32[24,8]{0,1:T(8,128)}, u32[]{:S(2)}) copy-start(f32[24,8]{0,1:T(8,128)} %param.14) | copy-start | bytes 2308
  449.7 8.7 %copy-start.5 = (bf16[4,4,8192]{2,1,0:T(4,128)(2,1)S(1)}, bf16[4,4,8192]{2,1,0:T(4,128)(2,1)}, u32[]{:S(2)}) copy-start(bf16[4,4,8192]{2,1,0:T(4,128)(2,1)} %param.18) | copy-start | bytes 786436
  449.7 9.7 %copy-start.3 = (bf16[4,256,512]{2,1,0:T(8,128)(2,1)S(1)}, bf16[4,256,512]{2,1,0:T(8,128)(2,1)}, u32[]{:S(2)}) copy-start(bf16[4,256,512]{2,1,0:T(8,128)(2,1)} %param.21) | copy-start | bytes 3145732
  449.7 58.0 %all-to-all-start.3 = ((bf16[64,4,4096]{2,1,0:T(4,128)(2,1)}), bf16[64,4,4096]{2,1,0:T(4,128)(2,1)}, u32[]{:S(2)}, u32[]{:S(2)}) async-start(bf16[64,4,4096]{2,1,0:T(4,128)(2,1)} %reshape.432), calls=%async_computation.3 | async-start | bytes 4194304 | tf_op jit(solution)/shard_map/all_to_all | solution.py:165
  458.3 1.5 copy-start.4
  459.5 0.7 copy-start.10
  459.5 0.7 copy-start.8
  461.9 2.2 copy-start.9
  510.3 6.9 %copy-start.1 = (bf16[24,4096]{1,0:T(8,128)(2,1)S(1)}, bf16[24,4096]{1,0:T(8,128)(2,1)}, u32[]{:S(2)}) copy-start(bf16[24,4096]{1,0:T(8,128)(2,1)} %param.12) | copy-start | bytes 589828
Sparse Core Ops, SparseCore 0:
  86.2 84.1 all-gather.2
  181.0 43.1 all-gather.4
Sparse Core Ops, SparseCore 1:
  202.1 208.5 all-reduce.3
where the time goes:
time: 528 us; the launch traced here: 525 us
  waiting for transfers between devices  282 us (53%)
  blocking collectives  109 us (21%)
  local copies, waits for them, and re-layouts  57.8 us (11%)
  matrix products  23.3 us (4%)
  between operations  21.1 us (4%)
  other arithmetic  16.2 us (3%)
  starting transfers between devices  15.9 us (3%)
    psum x1, waiting for transfers between devices, from_root(): return lax.psum(block, axis)  145 us
    all_gather x1, waiting for transfers between devices, per_device(): lax.all_gather(arrived, 'dp', axis=0, tiled=True)  75.7 us
    all_to_all x1, blocking collectives, per_device(): lax.all_to_all(outgoing.reshape(n_expert, experts_per * cap_rows, model_w...  61.6 us
    all_to_all x1, waiting for transfers between devices, per_device(): lax.all_to_all(expert_out, 'expert', split_axis=0, concat_axis=0, tiled=T...  39.3 us
    all_gather x1, blocking collectives, per_device(): lax.all_gather(hot_buffer.reshape(1, HOT, hot_rows, model_width), 'dp', a...  29.3 us
    all_gather x1, waiting for transfers between devices, per_device(): lax.all_gather(hidden_local, 'dp', axis=4, tiled=True)  22.1 us
    all_gather x1, blocking collectives, per_device(): lax.all_gather(hidden_hot, 'dp', axis=4, tiled=True)  17.8 us
    dot_general x2, matrix products, hidden_part(): jnp.einsum('qslcd,ldgf->qslcgf', rows, split_pair, preferred_element_type...  12.8 us
  transfers between devices with their start and end apart: 6, of which 4 were waited for; matrix products, arithmetic and copies ran while one was open for 12% of the time, Pallas kernels for 0%

commit v1 on v0

v1 whole, which is shorter than its diff:
```python
import math

import jax
import jax.numpy as jnp
from jax import lax
from jax.sharding import PartitionSpec as P

HEAD_DIM = 128
HOT = 2
CAP = 2
BF = jnp.bfloat16
F32 = jnp.float32


def attend_block(queries, draft_keys, draft_values, cache_keys, cache_values, cache_lengths):
    req_here, drafts, query_width = queries.shape
    context_len = cache_keys.shape[1]
    groups = draft_keys.shape[2] // HEAD_DIM
    per_group = query_width // (groups * HEAD_DIM)
    scaling = 1.0 / math.sqrt(HEAD_DIM)
    query_heads = queries.reshape(req_here, drafts, groups, per_group, HEAD_DIM)
    cache_k = cache_keys.reshape(req_here, context_len, groups, HEAD_DIM)
    cache_v = cache_values.reshape(req_here, context_len, groups, HEAD_DIM)
    draft_k = draft_keys.reshape(req_here, drafts, groups, HEAD_DIM)
    draft_v = draft_values.reshape(req_here, drafts, groups, HEAD_DIM)
    score_cache = (
        jnp.einsum("rigpe,rcge->rgpic", query_heads, cache_k, preferred_element_type=jnp.float32)
        * scaling
    )
    score_draft = (
        jnp.einsum("rigpe,rjge->rgpij", query_heads, draft_k, preferred_element_type=jnp.float32)
        * scaling
    )
    live_cache = jnp.arange(context_len, dtype=jnp.int32)[None, :] < cache_lengths[:, None]
    live_draft = (
        jnp.arange(drafts, dtype=jnp.int32)[None, :] <= jnp.arange(drafts, dtype=jnp.int32)[:, None]
    )
    score_cache = jnp.where(live_cache[:, None, None, None, :], score_cache, -1e30)
    score_draft = jnp.where(live_draft[None, None, None, :, :], score_draft, -1e30)
    highest = jnp.maximum(jnp.max(score_cache, axis=-1), jnp.max(score_draft, axis=-1))
    expo_cache = jnp.exp(score_cache - highest[..., None])
    expo_draft = jnp.exp(score_draft - highest[..., None])
    totals = jnp.sum(expo_cache, axis=-1) + jnp.sum(expo_draft, axis=-1)
    prob_cache = (expo_cache / totals[..., None]).astype(jnp.bfloat16)
    prob_draft = (expo_draft / totals[..., None]).astype(jnp.bfloat16)
    result = jnp.einsum(
        "rgpic,rcge->rigpe", prob_cache, cache_v, preferred_element_type=jnp.float32
    )
    result = result + jnp.einsum(
        "rgpij,rjge->rigpe", prob_draft, draft_v, preferred_element_type=jnp.float32
    )
    return result.astype(jnp.bfloat16).reshape(req_here, drafts, query_width)


def shift(x, k, n):
    return lax.ppermute(x, "dp", [(i, (i + k) % n) for i in range(n)])


def dot(a, b, dims):
    return lax.dot_general(a, b, (dims, ((), ())), preferred_element_type=F32)


def split3(x):
    hi = lax.reduce_precision(x, 8, 7)
    mid = lax.reduce_precision(x - hi, 8, 7)
    lo = x - hi - mid
    return [v.astype(BF) for v in (hi, mid, lo)]


def glu(gate_up):
    half = gate_up.shape[0] // 2
    return (jax.nn.silu(gate_up[:half]) * gate_up[half:]).astype(BF)


def per_device(
    tokens,
    route_ids,
    route_weights,
    placement,
    gate_up,
    down,
    queries,
    draft_keys,
    draft_values,
    cache_keys,
    cache_values,
    cache_lengths,
):
    n_dp = lax.axis_size("dp")
    n_expert = lax.axis_size("expert")
    me = lax.axis_index("dp")
    here = lax.axis_index("expert")
    rows, picks = route_ids.shape
    slots = placement.shape[0]
    per = gate_up.shape[0]
    width = tokens.shape[1]
    part = width // n_dp
    quarter = gate_up.shape[2] // 2
    chunk = n_dp * CAP

    slot_of = jnp.sum(
        (route_ids[:, :, None] == jnp.arange(slots, dtype=jnp.int32)) * placement, axis=2
    )
    own = jnp.sum(slot_of[:, :, None] == jnp.arange(slots, dtype=jnp.int32), axis=(0, 1))
    hot = own > CAP
    slot_range = jnp.arange(slots, dtype=jnp.int32)
    hot_slots = [
        jnp.min(jnp.where(hot, slot_range, slots - 1)),
        jnp.max(jnp.where(hot, slot_range, 0)),
    ]
    hot_gate, hot_down = [], []
    for one in hot_slots:
        mine = one // per == here
        gate_one = lax.dynamic_index_in_dim(gate_up, one % per, 0, keepdims=False)
        down_one = lax.dynamic_index_in_dim(down, one % per, 0, keepdims=False)
        hot_gate.append(jnp.where(mine, gate_one, jnp.zeros_like(gate_one)))
        hot_down.append(jnp.where(mine, down_one, jnp.zeros_like(down_one)))
    hot_gate, hot_down = lax.psum((hot_gate, hot_down), "expert")

    all_tokens = lax.all_gather(tokens, "dp", axis=0, tiled=True)
    all_ids = lax.all_gather(slot_of, "dp", axis=0, tiled=True)
    all_weights = lax.all_gather(route_weights, "dp", axis=0, tiled=True)
    all_rows = n_dp * rows
    my_part = lax.dynamic_slice_in_dim(all_tokens, me * part, part, axis=1)

    gate_up_t, _ = lax.optimization_barrier((gate_up, all_tokens))
    pieces = [lax.dynamic_slice_in_dim(gate_up_t, me * part, part, axis=1)]
    for k in range(1, n_dp):
        to_send = lax.dynamic_slice_in_dim(gate_up_t, (me + k) % n_dp * part, part, axis=1)
        pieces.append(shift(to_send, k, n_dp))

    match = all_ids[:, :, None] == slot_range
    takes = jnp.any(match, axis=1)
    weight_of = jnp.sum(jnp.where(match, all_weights[:, :, None], 0.0), axis=1)
    takes_plane = takes.reshape(n_dp, rows, slots).astype(jnp.int32)
    rank = (jnp.cumsum(takes_plane, axis=1) - takes_plane).reshape(all_rows, slots)
    plane_of = jnp.arange(all_rows, dtype=jnp.int32) // rows
    code = jnp.where(takes & ~hot[None, :], plane_of[:, None] * CAP + rank, -1)
    place = code.T[:, None, :] == jnp.arange(chunk, dtype=jnp.int32)[None, :, None]
    place = place.reshape(slots * chunk, all_rows)
    combine = jnp.where(place, jnp.repeat(weight_of.T, chunk, axis=0), 0.0)

    outgoing = dot(place.astype(BF), my_part, ((1,), (0,))).astype(BF)
    arrived = lax.all_to_all(
        outgoing.reshape(n_expert, per * chunk, part), "expert", 0, 0, tiled=True
    )
    returned = []
    results = []
    for s in range(per):
        x = arrived[:, s * chunk : (s + 1) * chunk].reshape(n_expert * chunk, part)
        total = dot(pieces[0][s], x, ((0,), (1,)))
        for k in range(1, n_dp):
            partial = dot(pieces[k][s], x, ((0,), (1,))).astype(BF)
            total = total + shift(partial, n_dp - k, n_dp).astype(F32)
        hidden = glu(total)
        out = None
        for k in range(n_dp):
            piece = hidden if k == 0 else shift(hidden, k, n_dp)
            down_piece = lax.dynamic_slice_in_dim(
                down[s], (me + n_dp - k) % n_dp * quarter, quarter, axis=0
            )
            term = dot(piece, down_piece, ((0,), (0,)))
            out = term if out is None else out + term
        results.append(out.astype(BF).reshape(n_expert, chunk, part))
    back = lax.all_to_all(jnp.concatenate(results, axis=1), "expert", 0, 0, tiled=True)
    back = back.reshape(slots * chunk, part)

    mixed = sum(dot(c, back, ((0,), (0,))) for c in split3(combine))

    for h in range(HOT):
        hidden = glu(dot(hot_gate[h], all_tokens, ((0,), (1,))))
        hidden = lax.all_gather(hidden, "dp", axis=0, tiled=True)
        out = dot(hidden, hot_down[h], ((0,), (0,))).astype(BF).astype(F32)
        hot_weight = jnp.sum(jnp.where(slot_range == hot_slots[h], weight_of, 0.0), axis=1)
        mixed = mixed + hot_weight[:, None] * out

    mixed = mixed.astype(BF).reshape(n_dp, rows, part)
    mixed = lax.all_to_all(mixed, "dp", 0, 0, tiled=True)
    mixed = jnp.transpose(mixed, (1, 0, 2)).reshape(rows, width)
    context = attend_block(
        queries, draft_keys, draft_values, cache_keys, cache_values, cache_lengths
    )
    return (mixed, context)


def solution(mesh):
    in_specs = (
        P(("dp", "expert"), None),
        P(("dp", "expert"), None),
        P(("dp", "expert"), None),
        P(),
        P("expert", None, "dp"),
        P("expert", None, "dp"),
        P(("dp", "expert"), None, None),
        P(("dp", "expert"), None, None),
        P(("dp", "expert"), None, None),
        P(("dp", "expert"), None, None),
        P(("dp", "expert"), None, None),
        P(("dp", "expert")),
    )
    out_specs = (P(("dp", "expert"), None), P(("dp", "expert"), None, None))
    return jax.shard_map(
        per_device, mesh=mesh, in_specs=in_specs, out_specs=out_specs, check_vma=False
    )
```

time: 528 us -> 352 us (0.67)
  waiting for transfers between devices: 282 us -> 152 us
  blocking collectives: 109 us -> 62.8 us
  local copies, waits for them, and re-layouts: 57.8 us -> 14 us
  starting transfers between devices: 15.9 us -> 47.8 us
  matrix products: 23.3 us -> 38.1 us
    all_gather x2 -> x0, waiting for transfers between devices: 97.8 us -> none  [the longest x1 75.7 us: per_device(): lax.all_gather(arrived, 'dp', axis=0, tiled=True)]
    psum x1, waiting for transfers between devices: 145 us -> 76.5 us  [per_device(): hot_gate, hot_down = lax.psum((hot_gate, hot_down), 'expert')]
    ppermute x0 -> x15, waiting for transfers between devices: none -> 63.3 us  [shift(): return lax.ppermute(x, 'dp', [(i, (i + k) % n) for i in range(n)])]
    all_to_all x1 -> x0, blocking collectives: 61.6 us -> none  [per_device(): lax.all_to_all(outgoing.reshape(n_expert, experts_per * cap_rows, model_w...]
    all_to_all x3, waiting for transfers between devices: 39.3 us -> 11.8 us  [the longest x1 8.44 us: per_device(): lax.all_to_all(outgoing.reshape(n_expert, per * chunk, part), 'expert', 0...]
    ppermute x0 -> x15, starting transfers between devices: none -> 21.7 us  [shift(): return lax.ppermute(x, 'dp', [(i, (i + k) % n) for i in range(n)])]
    all_gather x2 -> x5, blocking collectives: 47.1 us -> 62.8 us  [the longest x2 24.7 us: per_device(): hidden = lax.all_gather(hidden, 'dp', axis=0, tiled=True)]
    dot_general x4 -> x24, matrix products: 19.3 us -> 32.3 us  [dot(): return lax.dot_general(a, b, (dims, ((), ())), preferred_element_type=F32)]
  transfers between devices with their start and end apart: 6 -> 19, of which waited for: 4 -> 12; matrix products, arithmetic and copies ran while one was open for 12% -> 17% of each run, Pallas kernels for 0% -> 0%
where the time goes in v1:
time: 352 us; the launch traced here: 351 us
  waiting for transfers between devices  152 us (43%)
  blocking collectives  62.8 us (18%)
  starting transfers between devices  47.8 us (14%)
  matrix products  38.1 us (11%)
  between operations  20 us (6%)
  other arithmetic  16.3 us (5%)
  local copies, waits for them, and re-layouts  14 us (4%)
    psum x1, waiting for transfers between devices, per_device(): hot_gate, hot_down = lax.psum((hot_gate, hot_down), 'expert')  76.5 us
    ppermute x15, waiting for transfers between devices, shift(): return lax.ppermute(x, 'dp', [(i, (i + k) % n) for i in range(n)])  63.3 us
    dot_general x24, matrix products, dot(): return lax.dot_general(a, b, (dims, ((), ())), preferred_element_type=F32)  32.3 us
    all_gather x2, blocking collectives, per_device(): hidden = lax.all_gather(hidden, 'dp', axis=0, tiled=True)  24.7 us
    ppermute x15, starting transfers between devices, shift(): return lax.ppermute(x, 'dp', [(i, (i + k) % n) for i in range(n)])  21.7 us
    all_gather x1, blocking collectives, per_device(): all_tokens = lax.all_gather(tokens, 'dp', axis=0, tiled=True)  14 us
    all_to_all x1, starting transfers between devices, per_device(): lax.all_to_all(outgoing.reshape(n_expert, per * chunk, part), 'expert', 0...  12.2 us
    all_gather x1, blocking collectives, per_device(): all_ids = lax.all_gather(slot_of, 'dp', axis=0, tiled=True)  12.1 us
  transfers between devices with their start and end apart: 19, of which 12 were waited for; matrix products, arithmetic and copies ran while one was open for 17% of the time, Pallas kernels for 0%

profile of v1, /device:TPU:2, one launch (start us, length us, event | category | flops | bytes accessed | tf_op | source)
XLA Modules:
  0.0 350.6 jit_solution(17017473092636403375)
XLA Ops:
  7.2 14.0 %all_gather.17 = bf16[96,4096]{1,0:T(8,128)(2,1)S(1)} all-gather(bf16[24,4096]{1,0:T(8,128)(2,1)} %param.12), channel_id=1, replica_groups=mesh['dp'=4,'expert'=64] {'dp'}, dimensions={0}, use_global_device_ids=true | all-gather | bytes 983040 | tf_op jit(solution)/shard_map/all_gather | solution.py:120
  21.2 0.8 copy.67
  22.0 1.2 select_reduce_fusion.1
  23.4 12.1 %all-gather = s32[4,24,8]{1,2,0:T(8,128)S(1)} all-gather(s32[1,24,8]{1,2,0:T(8,128)S(1)} %copy.68), channel_id=1, replica_groups=mesh['dp'=4,'expert'=64] {'dp'}, dimensions={0}, use_global_device_ids=true | all-gather | bytes 3840 | tf_op jit(solution)/shard_map/all_gather | solution.py:121
  36.2 2.1 convolution_convert_fusion
  38.3 12.2 %all-to-all-start = ((bf16[64,16,1024]{2,1,0:T(8,128)(2,1)}), bf16[64,16,1024]{2,1,0:T(8,128)(2,1)}, u32[]{:S(2)}, u32[]{:S(2)}) async-start(bf16[64,16,1024]{2,1,0:T(8,128)(2,1)} %bitcast.11), calls=%async_computation | async-start | bytes 4194304 | tf_op jit(solution)/shard_map/all_to_all | solution.py:144
  50.6 4.9 %constant_dynamic-slice_fusion.2 = (bf16[2,1024,384]{2,1,0:T(8,128)(2,1)}, bf16[2,1024,384]{2,1,0:T(8,128)(2,1)}, bf16[2,1024,384]{2,1,0:T(8,128)(2,1)}) fusion(bf16[2,4096,384]{2,1,0:T(8,128)(2,1)} %param.16, s32[]{:T(128)S(6)} %select_n.204, s32[]{:T(128)S(6)} %select_n.208, s32[]{:T(128)S(6)} %select_n.206), kind=kLoop, calls=%fused_computation.145 | loop fusion | bytes 9437196 | tf_op jit(solution)/shard_map/dynamic_slice | solution.py:129
  55.5 2.0 collective-permute-start
  57.5 2.7 collective-permute-start.2
  60.1 0.7 select_reduce_fusion.5
  66.3 6.0 %fusion.101 = (bf16[1,768,1024]{2,1,0:T(8,128)(2,1)}, bf16[1,768,1024]{2,1,0:T(8,128)(2,1)}, bf16[768,1024]{1,0:T(8,128)(2,1)}, bf16[768,1024]{1,0:T(8,128)(2,1)}) fusion(bf16[2,768,1024]{2,1,0:T(8,128)(2,1)} %param.17, s32[]{:T(128)S(6)} %select_n.230, pred[]{:T(512)S(6)} %eq.140, s32[]{:T(128)S(6)} %select_n.219, pred[]{:T(512)S(6)} %eq.137), kind=kLoop, calls=%fused_computation.164 | loop fusion | flops 1572864 | bytes 12582922 | tf_op jit(solution)/shard_map/slice | solution.py:160
  72.3 3.2 select_bitcast_fusion.1
  75.5 18.2 %collective-permute-done = bf16[2,1024,384]{2,1,0:T(8,128)(2,1)} collective-permute-done((bf16[2,1024,384]{2,1,0:T(8,128)(2,1)}, bf16[2,1024,384]{2,1,0:T(8,128)(2,1)}, u32[]{:S(2)}, u32[]{:S(2)}) %collective-permute-start) | collective-permute-done | bytes 1572896 | tf_op jit(solution)/shard_map/ppermute | solution.py:56
  93.7 8.4 %all-to-all-done = bf16[64,16,1024]{2,1,0:T(8,128)(2,1)} async-done(((bf16[64,16,1024]{2,1,0:T(8,128)(2,1)}), bf16[64,16,1024]{2,1,0:T(8,128)(2,1)}, u32[]{:S(2)}, u32[]{:S(2)}) %all-to-all-start) | async-done | bytes 2097184 | tf_op jit(solution)/shard_map/all_to_all | solution.py:144
  102.1 2.1 convolution_convert_fusion.6
  104.3 3.5 collective-permute-start.1
  107.7 20.9 %collective-permute-done.2 = bf16[2,1024,384]{2,1,0:T(8,128)(2,1)} collective-permute-done((bf16[2,1024,384]{2,1,0:T(8,128)(2,1)}, bf16[2,1024,384]{2,1,0:T(8,128)(2,1)}, u32[]{:S(2)}, u32[]{:S(2)}) %collective-permute-start.2) | collective-permute-done | bytes 1572896 | tf_op jit(solution)/shard_map/ppermute | solution.py:56
  128.6 2.1 convolution_convert_fusion.5
  130.7 1.0 collective-permute-start.3
  131.6 2.1 convolution_convert_fusion.4
  133.9 2.1 convolution_convert_fusion.2
  136.0 2.9 collective-permute-start.10
  138.9 2.1 convolution_convert_fusion.1
  141.0 1.6 collective-permute-start.11
  142.5 2.1 fusion.19
  144.6 2.1 fusion.18
  146.8 2.1 convolution_convert_fusion.3
  148.9 1.8 collective-permute-start.9
  150.7 2.1 collective-permute-done.5
  153.3 2.0 collective-permute-start.7
  155.2 6.0 %collective-permute-done.10 = bf16[384,512]{1,0:T(8,128)(2,1)S(1)} collective-permute-done((bf16[384,512]{1,0:T(8,128)(2,1)S(1)}, bf16[384,512]{1,0:T(8,128)(2,1)S(1)}, u32[]{:S(2)}, u32[]{:S(2)}) %collective-permute-start.10) | collective-permute-done | bytes 393248 | tf_op jit(solution)/shard_map/ppermute | solution.py:56
  161.3 6.7 %collective-permute-done.11 = bf16[384,512]{1,0:T(8,128)(2,1)S(1)} collective-permute-done((bf16[384,512]{1,0:T(8,128)(2,1)S(1)}, bf16[384,512]{1,0:T(8,128)(2,1)S(1)}, u32[]{:S(2)}, u32[]{:S(2)}) %collective-permute-start.11) | collective-permute-done | bytes 393248 | tf_op jit(solution)/shard_map/ppermute | solution.py:56
  168.3 1.1 collective-permute-start.12
  169.5 2.6 collective-permute-start.13
  173.1 0.8 collective-permute-done.6
  173.9 0.5 collective-permute-start.14
  174.9 3.2 collective-permute-done.7
  179.1 3.1 collective-permute-done.12
  182.6 2.2 collective-permute-done.13
  185.8 1.5 pad_maximum_fusion
  187.3 10.4 %all-to-all-start.1 = ((bf16[64,16,1024]{2,1,0:T(8,128)(2,1)}), bf16[64,16,1024]{2,1,0:T(8,128)(2,1)S(1)}, u32[]{:S(2)}, u32[]{:S(2)}) async-start(bf16[64,16,1024]{2,1,0:T(8,128)(2,1)} %pad_maximum_fusion), calls=%async_computation.1 | async-start | bytes 4194304 | tf_op jit(solution)/shard_map/all_to_all | solution.py:165
  197.8 11.9 %all-gather.1 = f32[4,24,8]{1,2,0:T(8,128)S(1)} all-gather(f32[1,24,8]{1,2,0:T(8,128)S(1)} %bitcast.170), channel_id=1, replica_groups=mesh['dp'=4,'expert'=64] {'dp'}, dimensions={0}, use_global_device_ids=true | all-gather | bytes 3840 | tf_op jit(solution)/shard_map/all_gather | solution.py:122
  210.2 1.0 reshape.250
  211.2 2.2 reshape.249
  213.4 2.2 reshape.252
  215.6 0.8 fusion.103
  216.4 1.8 fusion.102
  218.4 0.8 copy-done.4
  219.7 1.3 iota_compare_fusion.6
  221.1 1.1 fusion.78
  222.2 76.5 %all-reduce.3.cloned.1.call-done = (bf16[4096,384]{1,0:T(8,128)(2,1)}, bf16[768,1024]{1,0:T(8,128)(2,1)}, bf16[4096,384]{1,0:T(8,128)(2,1)}, bf16[768,1024]{1,0:T(8,128)(2,1)}) async-done(((bf16[4096,384]{1,0:T(8,128)(2,1)}, bf16[768,1024]{1,0:T(8,128)(2,1)}, bf16[4096,384]{1,0:T(8,128)(2,1)}, bf16[768,1024]{1,0:T(8,128)(2,1)}), (bf16[4096,384]{1,0:T(8,128)(2,1)}, bf16[768,1024]{1,0:T(8,128)(2,1)}, ...) | async-done | bytes 9437200 | tf_op jit(solution)/shard_map/psum | solution.py:118
  298.7 2.5 fusion.104
  301.5 2.5 fusion.105
  304.2 12.6 %all_gather.18 = bf16[768,96]{1,0:T(8,128)(2,1)S(1)} all-gather(bf16[192,96]{1,0:T(8,128)(2,1)S(1)} %copy.75), channel_id=1, replica_groups=mesh['dp'=4,'expert'=64] {'dp'}, dimensions={0}, use_global_device_ids=true | all-gather | bytes 184320 | tf_op jit(solution)/shard_map/all_gather | solution.py:172
  316.8 12.1 %all_gather.19 = bf16[768,96]{1,0:T(8,128)(2,1)S(1)} all-gather(bf16[192,96]{1,0:T(8,128)(2,1)S(1)} %copy.76), channel_id=1, replica_groups=mesh['dp'=4,'expert'=64] {'dp'}, dimensions={0}, use_global_device_ids=true | all-gather | bytes 184320 | tf_op jit(solution)/shard_map/all_gather | solution.py:172
  328.9 1.8 fusion.9
  331.2 0.5 fusion.59
  331.7 0.5 convolution_add_fusion.2
  332.2 1.2 fusion.5
  333.4 3.4 all-to-all-start.2
  336.8 2.1 fusion.10
  339.0 0.8 reshape.254
  339.7 3.3 all-to-all-done.2
  343.1 0.7 copy.97
  (77 shorter events, 7.6 us)
Async XLA Ops:
  7.2 214.0 %copy-start = (bf16[4,4,512]{2,1,0:T(4,128)(2,1)S(1)}, bf16[4,4,512]{2,1,0:T(4,128)(2,1)}, u32[]{:S(2)}) copy-start(bf16[4,4,512]{2,1,0:T(4,128)(2,1)} %param.20) | copy-start | bytes 49156
  38.3 63.9 %all-to-all-start = ((bf16[64,16,1024]{2,1,0:T(8,128)(2,1)}), bf16[64,16,1024]{2,1,0:T(8,128)(2,1)}, u32[]{:S(2)}, u32[]{:S(2)}) async-start(bf16[64,16,1024]{2,1,0:T(8,128)(2,1)} %bitcast.11), calls=%async_computation | async-start | bytes 4194304 | tf_op jit(solution)/shard_map/all_to_all | solution.py:144
  50.5 248.2 %all-reduce.3.cloned.1.call-start = ((), (), s32[]{:S(2)}) async-start(), calls=%async_computation.3 | async-start | bytes 18874368 | tf_op jit(solution)/shard_map/psum | solution.py:118
  50.6 21.7 %slice-start = ((s8[6291456]{0:T(1024)(128)(4,1)}), s8[2097152]{0:T(1024)(128)(4,1)S(1)}, s32[]{:S(2)}) async-start(s8[6291456]{0:T(1024)(128)(4,1)} %bitcast.157), calls=%async_computation.4 | async-start | bytes 4194304
  55.5 38.2 %collective-permute-start = (bf16[2,1024,384]{2,1,0:T(8,128)(2,1)}, bf16[2,1024,384]{2,1,0:T(8,128)(2,1)}, u32[]{:S(2)}, u32[]{:S(2)}) collective-permute-start(bf16[2,1024,384]{2,1,0:T(8,128)(2,1)} %get-tuple-element.12), channel_id=1, source_target_pairs={{0,64},{64,128},{128,192},{192,0},{1,65},{65,129},{129,193},{193,1... | collective-permute-start | bytes 4718600 | tf_op jit(solution)/shard_map/ppermute | solution.py:56
  57.5 71.1 %collective-permute-start.2 = (bf16[2,1024,384]{2,1,0:T(8,128)(2,1)}, bf16[2,1024,384]{2,1,0:T(8,128)(2,1)}, u32[]{:S(2)}, u32[]{:S(2)}) collective-permute-start(bf16[2,1024,384]{2,1,0:T(8,128)(2,1)} %get-tuple-element.14), channel_id=1, source_target_pairs={{0,128},{64,192},{128,0},{192,64},{1,129},{65,193},{129,1},{193,65... | collective-permute-start | bytes 4718600 | tf_op jit(solution)/shard_map/ppermute | solution.py:56
  60.1 71.5 %collective-permute-start.4 = (bf16[2,1024,384]{2,1,0:T(8,128)(2,1)}, bf16[2,1024,384]{2,1,0:T(8,128)(2,1)}, u32[]{:S(2)}, u32[]{:S(2)}) collective-permute-start(bf16[2,1024,384]{2,1,0:T(8,128)(2,1)} %get-tuple-element.13), channel_id=1, source_target_pairs={{0,192},{64,0},{128,64},{192,128},{1,193},{65,1},{129,65},{193,129... | collective-permute-start | bytes 4718600 | tf_op jit(solution)/shard_map/ppermute | solution.py:56
  66.3 6.0 %slice-start.1 = ((s8[6291456]{0:T(1024)(128)(4,1)}), s8[4194304]{0:T(1024)(128)(4,1)S(1)}, s32[]{:S(2)}) async-start(s8[6291456]{0:T(1024)(128)(4,1)} %bitcast.157), calls=%async_computation.5 | async-start | bytes 8388608
  104.3 44.7 %collective-permute-start.1 = (bf16[384,512]{1,0:T(8,128)(2,1)S(1)}, bf16[384,512]{1,0:T(8,128)(2,1)S(1)}, u32[]{:S(2)}, u32[]{:S(2)}) collective-permute-start(bf16[384,512]{1,0:T(8,128)(2,1)S(1)} %convolution_convert_fusion.6), channel_id=1, source_target_pairs={{0,192},{64,0},{128,64},{192,128},{1,193},{65,1},{129,65},{193,129... | collective-permute-start | bytes 1179656 | tf_op jit(solution)/shard_map/ppermute | solution.py:56
  130.7 20.0 %collective-permute-start.3 = (bf16[384,512]{1,0:T(8,128)(2,1)S(1)}, bf16[384,512]{1,0:T(8,128)(2,1)S(1)}, u32[]{:S(2)}, u32[]{:S(2)}) collective-permute-start(bf16[384,512]{1,0:T(8,128)(2,1)S(1)} %convolution_convert_fusion.5), channel_id=1, source_target_pairs={{0,128},{64,192},{128,0},{192,64},{1,129},{65,193},{129,1},{193,65... | collective-permute-start | bytes 1179656 | tf_op jit(solution)/shard_map/ppermute | solution.py:56
  133.8 19.1 %collective-permute-start.5 = (bf16[384,512]{1,0:T(8,128)(2,1)S(1)}, bf16[384,512]{1,0:T(8,128)(2,1)S(1)}, u32[]{:S(2)}, u32[]{:S(2)}) collective-permute-start(bf16[384,512]{1,0:T(8,128)(2,1)S(1)} %convolution_convert_fusion.4), channel_id=1, source_target_pairs={{0,64},{64,128},{128,192},{192,0},{1,65},{65,129},{129,193},{193,1... | collective-permute-start | bytes 1179656 | tf_op jit(solution)/shard_map/ppermute | solution.py:56
  136.0 25.3 %collective-permute-start.10 = (bf16[384,512]{1,0:T(8,128)(2,1)S(1)}, bf16[384,512]{1,0:T(8,128)(2,1)S(1)}, u32[]{:S(2)}, u32[]{:S(2)}) collective-permute-start(bf16[384,512]{1,0:T(8,128)(2,1)S(1)} %convolution_convert_fusion.2), channel_id=1, source_target_pairs={{0,128},{64,192},{128,0},{192,64},{1,129},{65,193},{129,1},{193,65... | collective-permute-start | bytes 1179656 | tf_op jit(solution)/shard_map/ppermute | solution.py:56
  141.0 27.0 %collective-permute-start.11 = (bf16[384,512]{1,0:T(8,128)(2,1)S(1)}, bf16[384,512]{1,0:T(8,128)(2,1)S(1)}, u32[]{:S(2)}, u32[]{:S(2)}) collective-permute-start(bf16[384,512]{1,0:T(8,128)(2,1)S(1)} %convolution_convert_fusion.1), channel_id=1, source_target_pairs={{0,64},{64,128},{128,192},{192,0},{1,65},{65,129},{129,193},{193,1... | collective-permute-start | bytes 1179656 | tf_op jit(solution)/shard_map/ppermute | solution.py:56
  148.9 19.1 %collective-permute-start.9 = (bf16[384,512]{1,0:T(8,128)(2,1)S(1)}, bf16[384,512]{1,0:T(8,128)(2,1)S(1)}, u32[]{:S(2)}, u32[]{:S(2)}) collective-permute-start(bf16[384,512]{1,0:T(8,128)(2,1)S(1)} %convolution_convert_fusion.3), channel_id=1, source_target_pairs={{0,192},{64,0},{128,64},{192,128},{1,193},{65,1},{129,65},{193,129... | collective-permute-start | bytes 1179656 | tf_op jit(solution)/shard_map/ppermute | solution.py:56
  153.2 19.0 %copy-start.2 = (bf16[1,768,1024]{2,1,0:T(8,128)(2,1)S(1)}, bf16[1,768,1024]{2,1,0:T(8,128)(2,1)}, u32[]{:S(2)}) copy-start(bf16[1,768,1024]{2,1,0:T(8,128)(2,1)} %get-tuple-element.17) | copy-start | bytes 4718596
  153.2 20.7 %collective-permute-start.6 = (bf16[192,512]{1,0:T(8,128)(2,1)S(1)}, bf16[192,512]{1,0:T(8,128)(2,1)S(1)}, u32[]{:S(2)}, u32[]{:S(2)}) collective-permute-start(bf16[192,512]{1,0:T(8,128)(2,1)S(1)} %fusion.24), channel_id=1, source_target_pairs={{0,64},{64,128},{128,192},{192,0},{1,65},{65,129},{129,193},{193,1... | collective-permute-start | bytes 589832 | tf_op jit(solution)/shard_map/ppermute | solution.py:56
  153.3 24.8 %collective-permute-start.7 = (bf16[192,512]{1,0:T(8,128)(2,1)S(1)}, bf16[192,512]{1,0:T(8,128)(2,1)S(1)}, u32[]{:S(2)}, u32[]{:S(2)}) collective-permute-start(bf16[192,512]{1,0:T(8,128)(2,1)S(1)} %fusion.24), channel_id=1, source_target_pairs={{0,128},{64,192},{128,0},{192,64},{1,129},{65,193},{129,1},{193,65... | collective-permute-start | bytes 589832 | tf_op jit(solution)/shard_map/ppermute | solution.py:56
  161.3 17.3 %collective-permute-start.8 = (bf16[192,512]{1,0:T(8,128)(2,1)S(1)}, bf16[192,512]{1,0:T(8,128)(2,1)S(1)}, u32[]{:S(2)}, u32[]{:S(2)}) collective-permute-start(bf16[192,512]{1,0:T(8,128)(2,1)S(1)} %fusion.24), channel_id=1, source_target_pairs={{0,192},{64,0},{128,64},{192,128},{1,193},{65,1},{129,65},{193,129... | collective-permute-start | bytes 589832 | tf_op jit(solution)/shard_map/ppermute | solution.py:56
  168.2 4.4 %copy-start.1 = (bf16[1,768,1024]{2,1,0:T(8,128)(2,1)S(1)}, bf16[1,768,1024]{2,1,0:T(8,128)(2,1)}, u32[]{:S(2)}) copy-start(bf16[1,768,1024]{2,1,0:T(8,128)(2,1)} %get-tuple-element.18) | copy-start | bytes 4718596
  168.3 13.8 %collective-permute-start.12 = (bf16[192,512]{1,0:T(8,128)(2,1)S(1)}, bf16[192,512]{1,0:T(8,128)(2,1)S(1)}, u32[]{:S(2)}, u32[]{:S(2)}) collective-permute-start(bf16[192,512]{1,0:T(8,128)(2,1)S(1)} %fusion.23), channel_id=1, source_target_pairs={{0,64},{64,128},{128,192},{192,0},{1,65},{65,129},{129,193},{193,1... | collective-permute-start | bytes 589832 | tf_op jit(solution)/shard_map/ppermute | solution.py:56
  169.5 15.4 %collective-permute-start.13 = (bf16[192,512]{1,0:T(8,128)(2,1)S(1)}, bf16[192,512]{1,0:T(8,128)(2,1)S(1)}, u32[]{:S(2)}, u32[]{:S(2)}) collective-permute-start(bf16[192,512]{1,0:T(8,128)(2,1)S(1)} %fusion.23), channel_id=1, source_target_pairs={{0,128},{64,192},{128,0},{192,64},{1,129},{65,193},{129,1},{193,65... | collective-permute-start | bytes 589832 | tf_op jit(solution)/shard_map/ppermute | solution.py:56
  173.9 11.4 %collective-permute-start.14 = (bf16[192,512]{1,0:T(8,128)(2,1)S(1)}, bf16[192,512]{1,0:T(8,128)(2,1)S(1)}, u32[]{:S(2)}, u32[]{:S(2)}) collective-permute-start(bf16[192,512]{1,0:T(8,128)(2,1)S(1)} %fusion.23), channel_id=1, source_target_pairs={{0,192},{64,0},{128,64},{192,128},{1,193},{65,1},{129,65},{193,129... | collective-permute-start | bytes 589832 | tf_op jit(solution)/shard_map/ppermute | solution.py:56
  187.3 10.5 %copy-start.7 = (f32[24,8]{0,1:T(8,128)S(1)}, f32[24,8]{0,1:T(8,128)}, u32[]{:S(2)}) copy-start(f32[24,8]{0,1:T(8,128)} %param.14) | copy-start | bytes 2308
  187.3 22.9 %copy-start.5 = (bf16[4,4,8192]{2,1,0:T(4,128)(2,1)S(1)}, bf16[4,4,8192]{2,1,0:T(4,128)(2,1)}, u32[]{:S(2)}) copy-start(bf16[4,4,8192]{2,1,0:T(4,128)(2,1)} %param.18) | copy-start | bytes 786436
  187.3 143.8 %all-to-all-start.1 = ((bf16[64,16,1024]{2,1,0:T(8,128)(2,1)}), bf16[64,16,1024]{2,1,0:T(8,128)(2,1)S(1)}, u32[]{:S(2)}, u32[]{:S(2)}) async-start(bf16[64,16,1024]{2,1,0:T(8,128)(2,1)} %pad_maximum_fusion), calls=%async_computation.1 | async-start | bytes 4194304 | tf_op jit(solution)/shard_map/all_to_all | solution.py:165
  211.2 4.4 %copy-start.9 = (s32[4]{0:T(128)S(1)}, s32[4]{0:T(128)}, u32[]{:S(2)}) copy-start(s32[4]{0:T(128)} %param.23) | copy-start | bytes 52
  211.2 4.5 %copy-start.6 = (bf16[4,4,4,16,128]{4,3,2,1,0:T(8,128)(2,1)S(1)}, bf16[4,4,4,16,128]{4,3,2,1,0:T(8,128)(2,1)}, u32[]{:S(2)}) copy-start(bf16[4,4,4,16,128]{4,3,2,1,0:T(8,128)(2,1)} %reshape.250) | copy-start | bytes 786436
  211.2 4.5 %copy-start.8 = (bf16[4,4,512]{2,1,0:T(4,128)(2,1)S(1)}, bf16[4,4,512]{2,1,0:T(4,128)(2,1)}, u32[]{:S(2)}) copy-start(bf16[4,4,512]{2,1,0:T(4,128)(2,1)} %param.19) | copy-start | bytes 49156
  218.2 1.0 copy-start.4
  304.2 26.5 %copy-start.3 = (bf16[768,1024]{1,0:T(8,128)(2,1)S(1)}, bf16[768,1024]{1,0:T(8,128)(2,1)}, u32[]{:S(2)}) copy-start(bf16[768,1024]{1,0:T(8,128)(2,1)} %get-tuple-element.9) | copy-start | bytes 4718596
  333.4 9.7 %all-to-all-start.2 = ((bf16[4,24,1024]{2,1,0:T(8,128)(2,1)}), bf16[4,24,1024]{2,1,0:T(8,128)(2,1)S(1)}, u32[]{:S(2)}, u32[]{:S(2)}) async-start(bf16[4,24,1024]{2,1,0:T(8,128)(2,1)} %bitcast.38), calls=%async_computation.2 | async-start | bytes 393216 | tf_op jit(solution)/shard_map/all_to_all | solution.py:178
Sparse Core Ops, SparseCore 0:
  75.6 223.0 all-reduce.2
